TPU v7x, 512 devices: a whole 4x4x16 slice. The times are simulated.
512 devices in a mesh: ctx: 32 (over z, core), head: 4 (over y), dp: 4 (over x).
Axes of the slice: x: 4, y: 4, z: 16, core: 2. Of those that a mesh axis runs over, the one named last changes fastest.
Arguments:
- latent: bfloat16 [4, 4096, 576], P('dp', 'ctx'), may hold values from -6 to 6
- queries: bfloat16 [4, 4096, 12288], P('dp', 'ctx', 'head'), may hold values from -330 to 330
- out_grad: bfloat16 [4, 4096, 8192], P('dp', 'ctx', 'head'), may hold values from -6 to 6
- segment_ids: int32 [4, 4096], P('dp', 'ctx'), may hold values from 0 to 31, never falling along the last dimension, each value on 1 to 256 neighbouring positions
- key_up: bfloat16 [512, 8192], P('dp', 'head'), may hold values from -0.25 to 0.25
- value_up: bfloat16 [512, 8192], P('dp', 'head'), may hold values from -0.25 to 0.25
Outputs:
- query_grad: bfloat16 [4, 4096, 12288], P('dp', 'ctx', 'head')
- latent_grad: bfloat16 [4, 4096, 576], P('dp', 'ctx')
- key_up_grad: float32 [512, 8192], P(('ctx', 'dp'), 'head')
Inputs may be any that keep to these rules, and one draw needn't show every extreme that they name: `segment_ids`: segment numbers never fall along a trajectory; each segment holds at most 256 positions and one holds exactly 256.
All inputs are finite; a program needn't handle non-finite values.
Results may differ from a plain program's by a relative error of at most 0.0072.
Values may be sent and summed in bfloat16 or wider, within the bound.
A program may use at most 64 MiB of HBM per device.

v0:
```python
import jax
import jax.numpy as jnp
from jax import lax
from jax.sharding import PartitionSpec as P

D_NOPE = 128


def shifted(x, axis, by):
    size = lax.axis_size(axis)
    pairs = [(i, i + by) for i in range(size) if 0 <= i + by < size]
    return lax.ppermute(x, axis, pairs)


def attend(query_block, grad_block, key_window, value_window, rope_window, allowed, score_scale):
    nope_width = value_window.shape[-1]
    query_nope = query_block[:, :, :nope_width]
    query_rope = query_block[:, :, nope_width:]
    scores = (
        jnp.einsum("ihd,jhd->hij", query_nope, key_window, preferred_element_type=jnp.float32)
        + jnp.einsum("ihd,jd->hij", query_rope, rope_window, preferred_element_type=jnp.float32)
    ) * score_scale
    scores = jnp.where(allowed[None], scores, -1e30)
    row_max = jnp.max(scores, axis=-1, keepdims=True)
    numerator = jnp.exp(scores - row_max)
    weights = numerator / jnp.sum(numerator, axis=-1, keepdims=True)
    weights_low = weights.astype(jnp.bfloat16)
    attended = jnp.einsum(
        "hij,jhd->ihd", weights_low, value_window, preferred_element_type=jnp.float32
    )
    out_dot = jnp.sum(grad_block.astype(jnp.float32) * attended, axis=-1)
    prob_grad = jnp.einsum(
        "ihd,jhd->hij", grad_block, value_window, preferred_element_type=jnp.float32
    )
    score_grad = (score_scale * weights * (prob_grad - jnp.transpose(out_dot)[:, :, None])).astype(
        jnp.bfloat16
    )
    query_grad = jnp.concatenate(
        [
            jnp.einsum("hij,jhd->ihd", score_grad, key_window, preferred_element_type=jnp.float32),
            jnp.einsum("hij,jd->ihd", score_grad, rope_window, preferred_element_type=jnp.float32),
        ],
        axis=-1,
    )
    key_grad = jnp.einsum(
        "hij,ihd->jhd", score_grad, query_nope, preferred_element_type=jnp.float32
    ).astype(jnp.bfloat16)
    rope_grad = jnp.einsum(
        "hij,ihd->jd", score_grad, query_rope, preferred_element_type=jnp.float32
    )
    value_grad = jnp.einsum(
        "hij,ihd->jhd", weights_low, grad_block, preferred_element_type=jnp.float32
    ).astype(jnp.bfloat16)
    return (query_grad, key_grad, value_grad, rope_grad)


def window_mask(query_segments, key_segments, first_key, first_query):
    query_positions = first_query + jnp.arange(query_segments.shape[0], dtype=jnp.int32)
    key_positions = first_key + jnp.arange(key_segments.shape[0], dtype=jnp.int32)
    causal = (key_positions[None, :] <= query_positions[:, None]) & (key_positions[None, :] >= 0)
    return causal & (key_segments[None, :] == query_segments[:, None])


def local(latent, queries, out_grad, segment_ids, key_up, value_up):
    tok_rows = latent.shape[1]
    reach_blocks = min(2, lax.axis_size("ctx") - 1)
    ctx_index = lax.axis_index("ctx")
    w_key, w_value = (
        lax.all_gather(key_up, "dp", axis=0, tiled=True),
        lax.all_gather(value_up, "dp", axis=0, tiled=True),
    )
    latent_width = w_key.shape[0]
    head_columns = w_key.shape[1]
    nope_width = D_NOPE
    head_count = head_columns // nope_width
    rope_width = latent.shape[2] - latent_width
    score_scale = (nope_width + rope_width) ** (-0.5)
    window_rows = (reach_blocks + 1) * tok_rows
    own_start = reach_blocks * tok_rows
    own_latent = latent[0]
    own_segments = segment_ids[0]
    query_block = queries[0].reshape(tok_rows, head_count, nope_width + rope_width)
    grad_block = out_grad[0].reshape(tok_rows, head_count, nope_width)
    fetched = [
        shifted((own_latent, own_segments), "ctx", offset) for offset in range(reach_blocks, 0, -1)
    ]
    latent_window = jnp.concatenate([item[0] for item in fetched] + [own_latent], axis=0)
    key_segments = jnp.concatenate([item[1] for item in fetched] + [own_segments], axis=0)
    compressed = latent_window[:, :latent_width]
    key_window = (
        jnp.dot(compressed, w_key, preferred_element_type=jnp.float32)
        .astype(jnp.bfloat16)
        .reshape(window_rows, head_count, nope_width)
    )
    value_window = (
        jnp.dot(compressed, w_value, preferred_element_type=jnp.float32)
        .astype(jnp.bfloat16)
        .reshape(window_rows, head_count, nope_width)
    )
    rope_window = latent_window[:, latent_width:]
    allowed = window_mask(
        own_segments, key_segments, (ctx_index - reach_blocks) * tok_rows, ctx_index * tok_rows
    )
    query_grad, key_grad, value_grad, rope_grad = attend(
        query_block, grad_block, key_window, value_window, rope_window, allowed, score_scale
    )
    key_grad = key_grad.reshape(window_rows, head_columns)
    value_grad = value_grad.reshape(window_rows, head_columns)
    contract = (((1,), (1,)), ((), ()))
    latent_terms = jnp.concatenate(
        [
            lax.dot_general(key_grad, w_key, contract, preferred_element_type=jnp.float32)
            + lax.dot_general(value_grad, w_value, contract, preferred_element_type=jnp.float32),
            rope_grad,
        ],
        axis=1,
    )
    total_grad = latent_terms[own_start:]
    for offset in range(1, reach_blocks + 1):
        first = (reach_blocks - offset) * tok_rows
        total_grad = total_grad + shifted(
            latent_terms[first : first + tok_rows].astype(jnp.bfloat16), "ctx", -offset
        ).astype(jnp.float32)
    total_grad = lax.psum(total_grad, "head")
    key_up_grad = lax.psum_scatter(
        lax.dot_general(
            compressed, key_grad, (((0,), (0,)), ((), ())), preferred_element_type=jnp.float32
        ),
        ("ctx", "dp"),
        scatter_dimension=0,
        tiled=True,
    )
    query_out = query_grad.astype(jnp.bfloat16).reshape(
        tok_rows, head_count * (nope_width + rope_width)
    )
    return (query_out[None], total_grad.astype(jnp.bfloat16)[None], key_up_grad)


def solution(mesh):
    return jax.shard_map(
        local,
        mesh=mesh,
        in_specs=(
            P("dp", "ctx", None),
            P("dp", "ctx", "head"),
            P("dp", "ctx", "head"),
            P("dp", "ctx"),
            P("dp", "head"),
            P("dp", "head"),
        ),
        out_specs=(P("dp", "ctx", "head"), P("dp", "ctx", None), P(("ctx", "dp"), "head")),
        check_vma=False,
    )
```

profile of v0, /device:TPU:1, one launch (start us, length us, event | category | flops | bytes accessed | tf_op | source)
XLA Modules:
  0.0 487.1 jit_solution(10151927938640826887)
XLA Ops:
  8.7 4.9 %collective-permute-start.1 = (bf16[128,576]{0,1:T(8,128)(2,1)}, bf16[128,576]{0,1:T(8,128)(2,1)S(1)}, u32[]{:S(2)}, u32[]{:S(2)}) collective-permute-start(bf16[128,576]{0,1:T(8,128)(2,1)} %bitcast.78), channel_id=1, source_target_pairs={{0,16},{16,32},{32,48},{48,64},{64,80},{80,96},{96,112},{112,128},... | collective-permute-start | bytes 442376 | tf_op jit(solution)/shard_map/ppermute | solution.py:12
  13.7 3.5 collective-permute-start
  17.2 2.2 collective-permute-start.3
  19.4 3.5 collective-permute-start.2
  23.0 2.1 copy.48
  25.5 1.3 dynamic-slice
  27.9 26.1 %all-gather.5.cloned.1.call-done = bf16[512,2048]{1,0:T(8,128)(2,1)} async-done(((bf16[128,2048]{1,0:T(8,128)(2,1)}), bf16[512,2048]{1,0:T(8,128)(2,1)}) %all-gather.5.cloned.1.call-update) | async-done | bytes 2097168 | tf_op jit(solution)/shard_map/all_gather | solution.py:70
  54.0 3.7 convolution_convert_fusion
  57.7 2.6 copy.75
  60.3 34.4 %all-gather.3.cloned.1.call-done = bf16[512,2048]{1,0:T(8,128)(2,1)} async-done(((bf16[128,2048]{1,0:T(8,128)(2,1)}), bf16[512,2048]{1,0:T(8,128)(2,1)}) %all-gather.3.cloned.1.call-update) | async-done | bytes 2097168 | tf_op jit(solution)/shard_map/all_gather | solution.py:69
  94.7 3.7 convolution_convert_fusion.1
  98.4 1.9 copy.74
  101.7 2.6 fusion.25
  104.2 5.3 %convolution_convert_fusion.2 = bf16[16,384,128]{1,2,0:T(8,128)(2,1)} fusion(bf16[128,16,128]{0,2,1:T(8,128)(2,1)} %bitcast.82, f32[16,128]{1,0:T(8,128)S(1)} %get-tuple-element.14, f32[16,128,384]{1,2,0:T(8,128)} %copy-done), kind=kOutput, calls=%fused_computation.9 | convolution fusion | flops 204474752 | bytes 5251072 | tf_op jit(solution)/shard_map/hij,ihd->jhd/dot_general | solution.py:51
  109.5 4.2 fusion.6
  113.7 3.5 fusion.1
  119.2 3.3 fusion.16
  122.5 3.2 fusion.26
  125.7 1.5 convolution_bitcast_fusion.1
  130.5 2.6 collective-permute-start.4
  136.4 2.7 collective-permute-done.4
  140.1 18.2 %all-reduce.5 = bf16[128,576]{1,0:T(8,128)(2,1)S(1)} all-reduce(f32[128,576]{1,0:T(8,128)S(1)} %fusion.15), channel_id=1, replica_groups=mesh['ctx'=32,'head'=4,'dp'=4] {'head'}, use_global_device_ids=true, to_apply=%region_3.4 | all-reduce | flops 73728 | bytes 442368 | tf_op jit(solution)/shard_map/psum | solution.py:124
  159.2 320.0 %all-reduce.4.cloned.1.call-done = f32[512,2048]{1,0:T(8,128)} async-done(((f32[512,2048]{1,0:T(8,128)}), f32[512,2048]{1,0:T(8,128)}) %all-reduce.4.cloned.1.call-update) | async-done | bytes 4194320
  479.1 1.5 constant_dynamic-slice_fusion
  (60 shorter events, 13.8 us)
Async XLA Ops:
  7.2 20.6 %copy-start.10 = (bf16[1,128,576]{1,2,0:T(8,128)(2,1)S(1)}, bf16[1,128,576]{1,2,0:T(8,128)(2,1)}, u32[]{:S(2)}) copy-start(bf16[1,128,576]{1,2,0:T(8,128)(2,1)} %param.6) | copy-start | bytes 442372
  7.2 20.3 %copy-start.11 = (s32[1,128]{1,0:T(1,128)S(1)}, s32[1,128]{1,0:T(1,128)}, u32[]{:S(2)}) copy-start(s32[1,128]{1,0:T(1,128)} %param.9) | copy-start | bytes 1540
  7.2 17.9 %copy-start.9 = (bf16[1,128,3072]{2,1,0:T(8,128)(2,1)S(1)}, bf16[1,128,3072]{2,1,0:T(8,128)(2,1)}, u32[]{:S(2)}) copy-start(bf16[1,128,3072]{2,1,0:T(8,128)(2,1)} %param.7) | copy-start | bytes 2359300
  7.2 46.8 %all-gather.5.cloned.1.call-start = ((), (), s32[]{:S(2)}) async-start(), calls=%async_computation.1 | async-start | bytes 2621440 | tf_op jit(solution)/shard_map/all_gather | solution.py:70
  7.9 86.8 %all-gather.3.cloned.1.call-start = ((), (), s32[]{:S(2)}) async-start(), calls=%async_computation | async-start | bytes 2621440 | tf_op jit(solution)/shard_map/all_gather | solution.py:69
  8.7 470.4 %all-reduce.4.cloned.1.call-start = ((), (), s32[]{:S(2)}) async-start(), calls=%async_computation.2 | async-start | bytes 8388608
  8.7 19.0 %collective-permute-start.1 = (bf16[128,576]{0,1:T(8,128)(2,1)}, bf16[128,576]{0,1:T(8,128)(2,1)S(1)}, u32[]{:S(2)}, u32[]{:S(2)}) collective-permute-start(bf16[128,576]{0,1:T(8,128)(2,1)} %bitcast.78), channel_id=1, source_target_pairs={{0,16},{16,32},{32,48},{48,64},{64,80},{80,96},{96,112},{112,128},... | collective-permute-start | bytes 442376 | tf_op jit(solution)/shard_map/ppermute | solution.py:12
  13.7 14.1 %collective-permute-start = (bf16[128,576]{0,1:T(8,128)(2,1)}, bf16[128,576]{0,1:T(8,128)(2,1)S(1)}, u32[]{:S(2)}, u32[]{:S(2)}) collective-permute-start(bf16[128,576]{0,1:T(8,128)(2,1)} %bitcast.79), channel_id=1, source_target_pairs={{0,32},{16,48},{32,64},{48,80},{64,96},{80,112},{96,128},{112,144}... | collective-permute-start | bytes 442376 | tf_op jit(solution)/shard_map/ppermute | solution.py:12
  17.2 10.3 %collective-permute-start.3 = (s32[128]{0:T(128)}, s32[128]{0:T(128)S(1)}, u32[]{:S(2)}, u32[]{:S(2)}) collective-permute-start(s32[128]{0:T(128)} %bitcast.85), channel_id=1, source_target_pairs={{0,16},{16,32},{32,48},{48,64},{64,80},{80,96},{96,112},{112,128},... | collective-permute-start | bytes 1544 | tf_op jit(solution)/shard_map/ppermute | solution.py:12
  19.4 8.1 %collective-permute-start.2 = (s32[128]{0:T(128)}, s32[128]{0:T(128)S(1)}, u32[]{:S(2)}, u32[]{:S(2)}) collective-permute-start(s32[128]{0:T(128)} %bitcast.86), channel_id=1, source_target_pairs={{0,32},{16,48},{32,64},{48,80},{64,96},{80,112},{96,128},{112,144}... | collective-permute-start | bytes 1544 | tf_op jit(solution)/shard_map/ppermute | solution.py:12
  25.5 75.4 %copy-start.2 = (bf16[1,128,3072]{1,2,0:T(8,128)(2,1)}, bf16[1,128,3072]{1,2,0:T(8,128)(2,1)S(1)}, u32[]{:S(2)}) copy-start(bf16[1,128,3072]{1,2,0:T(8,128)(2,1)S(1)} %copy.45) | copy-start | bytes 2359300
  27.9 66.8 %copy-start.6 = (bf16[384,576]{0,1:T(8,128)(2,1)}, bf16[384,576]{0,1:T(8,128)(2,1)S(1)}, u32[]{:S(2)}) copy-start(bf16[384,576]{0,1:T(8,128)(2,1)S(1)} %pad_maximum_fusion.2) | copy-start | bytes 1327108
  101.7 2.6 copy-start
  104.2 5.3 %copy-start.8 = (bf16[384,2048]{0,1:T(8,128)(2,1)S(1)}, bf16[384,2048]{0,1:T(8,128)(2,1)}, u32[]{:S(2)}) copy-start(bf16[384,2048]{0,1:T(8,128)(2,1)} %copy.75) | copy-start | bytes 4718596
  113.7 3.5 copy-start.3
  117.2 1.9 copy-start.7
  118.0 1.1 copy-start.1
  122.4 4.8 copy-start.12
  122.4 4.8 copy-start.13
  128.3 5.5 %copy-start.4 = (f32[384,512]{1,0:T(8,128)}, f32[384,512]{1,0:T(8,128)S(1)}, u32[]{:S(2)}) copy-start(f32[384,512]{1,0:T(8,128)S(1)} %convolution_add_fusion) | copy-start | bytes 2359300
  129.3 7.2 %collective-permute-start.5 = (bf16[128,576]{1,0:T(8,128)(2,1)}, bf16[128,576]{1,0:T(8,128)(2,1)S(1)}, u32[]{:S(2)}, u32[]{:S(2)}) collective-permute-start(bf16[128,576]{1,0:T(8,128)(2,1)} %get-tuple-element.13), channel_id=1, source_target_pairs={{32,0},{48,16},{64,32},{80,48},{96,64},{112,80},{128,96},{144,112}... | collective-permute-start | bytes 442376 | tf_op jit(solution)/shard_map/ppermute | solution.py:12
  130.5 8.6 %collective-permute-start.4 = (bf16[128,576]{1,0:T(8,128)(2,1)}, bf16[128,576]{1,0:T(8,128)(2,1)}, u32[]{:S(2)}, u32[]{:S(2)}) collective-permute-start(bf16[128,576]{1,0:T(8,128)(2,1)} %get-tuple-element.12), channel_id=1, source_target_pairs={{16,0},{32,16},{48,32},{64,48},{80,64},{96,80},{112,96},{128,112},... | collective-permute-start | bytes 442376 | tf_op jit(solution)/shard_map/ppermute | solution.py:12
  134.1 5.0 %copy-start.5 = (f32[384,512]{1,0:T(8,128)S(1)}, f32[384,512]{1,0:T(8,128)}, u32[]{:S(2)}) copy-start(f32[384,512]{1,0:T(8,128)} %copy-done.4) | copy-start | bytes 2359300
Sparse Core Ops, SparseCore 0:
  10.1 43.7 all-gather.4
  56.1 38.5 all-gather.2
  122.6 356.5 all-reduce.3
where the time goes:
time: 488 us; the launch traced here: 487 us
  waiting for transfers between devices  386 us (79%)
  matrix products  32.5 us (7%)
  starting transfers between devices  18.2 us (4%)
  blocking collectives  18.2 us (4%)
  between operations  14.8 us (3%)
  local copies, waits for them, and re-layouts  13.8 us (3%)
    unnamed x4, waiting for transfers between devices  321 us
    all_gather x1, waiting for transfers between devices, local(): lax.all_gather(key_up, 'dp', axis=0, tiled=True)  34.4 us
    all_gather x1, waiting for transfers between devices, local(): lax.all_gather(value_up, 'dp', axis=0, tiled=True)  26.1 us
    psum x1, blocking collectives, local(): total_grad = lax.psum(total_grad, 'head')  18.2 us
    ppermute x6, starting transfers between devices, shifted(): return lax.ppermute(x, axis, pairs)  18.1 us
  transfers between devices with their start and end apart: 9, of which 5 were waited for; matrix products, arithmetic and copies ran while one was open for 4% of the time, Pallas kernels for 0%

commit v1 on v0

v1 whole, which is shorter than its diff:
```python
import jax
import jax.numpy as jnp
from jax import lax
from jax.experimental import pallas as pl
from jax.experimental.pallas import tpu as pltpu
from jax.sharding import PartitionSpec as P

F32 = jnp.float32
BF16 = jnp.bfloat16
SCALE = (128 + 64) ** -0.5
N_REMOTE = 128
N_LOCAL = 40


def mm(a, b):
    return lax.dot_general(a, b, (((1,), (0,)), ((), ())), preferred_element_type=F32)


def mm_nt(a, b):
    return lax.dot_general(a, b, (((1,), (1,)), ((), ())), preferred_element_type=F32)


def mm_tn(a, b):
    return lax.dot_general(a, b, (((0,), (0,)), ((), ())), preferred_element_type=F32)


def rows(start, size):
    return pl.ds(pl.multiple_of(start, size), size)


def cols(start, size):
    return pl.ds(pl.multiple_of(start, 128), size)


def kernel(
    lat_in, qry_in, grd_in, seg_in, wk_in, wv_in,
    qg_out, lg_out, ku_out,
    wk, wv, qs, gs, lat, seg, bias, ctp, rope0, rope1, kx, vx, dq, u, lacc, racc, dkp, dvp,
    ra, rb, rla, rlb, rra, rrb, sa, sb, tb, za, zp, zb, lb, p1, l2, p2, fl,
    send_sem, recv_sem, local_sem,
):
    s = lax.axis_index("ctx")
    y = lax.axis_index("head")
    x = lax.axis_index("dp")
    z = s // 2
    c = s % 2
    oc = 1 - c
    par = z % 2
    n_z = lax.axis_size("ctx") // 2
    order = [par, 2 + par, 1 - par, 3 - par]

    def at(dz=0, core=None, x_to=None, y_to=None):
        core = c if core is None else core
        zt = (z + dz + n_z) % n_z
        return {
            "ctx": zt * 2 + core,
            "head": y if y_to is None else y_to,
            "dp": x if x_to is None else x_to,
        }

    right, left, far = (x + 1) % 4, (x + 3) % 4, (x + 2) % 4
    pair = at(core=oc)
    sends = []
    locals_ = []
    count = [0, 0]

    def push(src, dst, dev):
        i = count[0]
        count[0] += 1
        copy = pltpu.make_async_remote_copy(
            src_ref=src, dst_ref=dst, send_sem=send_sem.at[i], recv_sem=recv_sem.at[i],
            device_id=dev, device_id_type=pl.DeviceIdType.MESH,
        )
        copy.start()
        sends.append(copy)
        return copy

    def local(src, dst):
        i = count[1]
        count[1] += 1
        copy = pltpu.make_async_copy(src, dst, local_sem.at[i])
        copy.start()
        return copy

    l_lat = [local(lat_in, lat.at[rows((2 + c) * 128, 128)])]
    l_w, l_q = [], []
    for p in order:
        l_w.append((
            local(wk_in.at[:, cols(c * 1024 + p * 256, 256)], wk.at[p, rows(x * 128, 128)]),
            local(wv_in.at[:, cols(c * 1024 + p * 256, 256)], wv.at[p, rows(x * 128, 128)]),
        ))
        l_q.append((
            local(qry_in.at[:, cols(c * 1536 + p * 384, 384)], qs.at[p, rows(c * 128, 128)]),
            local(grd_in.at[:, cols(c * 1024 + p * 256, 256)], gs.at[p, rows(c * 128, 128)]),
        ))
    seg[2 + c] = seg_in[...]

    partners = [pair, at(x_to=right), at(x_to=left)]
    partners += [at(dz=d) for d in (1, -1, 2, -2)]
    partners += [at(dz=4 * d, core=(c if dc == 0 else oc)) for d in (1, 2, 3) for dc in (0, 1)]
    for dy in (1, 2, 3):
        yt = (y + dy) % 4
        partners += [at(y_to=yt), at(dz=-1, y_to=yt), at(dz=1, y_to=yt)]
    barrier = pltpu.get_barrier_semaphore()
    for dev in partners:
        pl.semaphore_signal(barrier, inc=1, device_id=dev, device_id_type=pl.DeviceIdType.MESH)
    pl.semaphore_wait(barrier, len(partners))

    def push_direct(k):
        p = order[k]
        out = []
        for w_in, w in ((wk_in, wk), (wv_in, wv)):
            src = w_in.at[:, cols(c * 1024 + p * 256, 256)]
            dst = w.at[p, rows(x * 128, 128)]
            out.append((push(src, dst, at(x_to=right)), push(src, dst, at(x_to=left))))
        return out

    direct = [push_direct(0)]
    lat_z = push(lat_in, lat.at[rows(c * 128, 128)], at(dz=1))
    seg_z = push(seg_in, seg.at[c], at(dz=1))
    lat_p = push(lat_in, lat.at[rows((2 + c) * 128, 128)], pair)
    seg_p = push(seg_in, seg.at[2 + c], pair)

    def push_tokens(k):
        p = order[k]
        return (
            push(qry_in.at[:, cols(oc * 1536 + p * 384, 384)], qs.at[p, rows(c * 128, 128)], pair),
            push(grd_in.at[:, cols(oc * 1024 + p * 256, 256)], gs.at[p, rows(c * 128, 128)], pair),
        )

    tokens = [push_tokens(0)]

    def forward_x(k):
        p = order[k]
        for pushed in direct[k]:
            for copy in pushed:
                copy.wait_recv()
        mine_k = wk.at[p, rows(left * 128, 128)]
        mine_v = wv.at[p, rows(right * 128, 128)]
        return push(mine_k, mine_k, at(x_to=right)), push(mine_v, mine_v, at(x_to=left))

    def forward_z(k):
        p = order[k]
        out = []
        for xs in (left, right, far):
            piece_k = wk.at[p, rows(xs * 128, 128)]
            piece_v = wv.at[p, rows(xs * 128, 128)]
            out.append(push(piece_k, piece_k, at(dz=1)))
            out.append(push(piece_v, piece_v, at(dz=-1)))
        return out

    lat_z.wait_recv()
    lat_f = push(lat.at[rows(c * 128, 128)], lat.at[rows(c * 128, 128)], pair)
    seg_z.wait_recv()
    seg_f = push(seg.at[c], seg.at[c], pair)

    xf0 = forward_x(0)
    direct.append(push_direct(1))
    for k in (1, 2, 3):
        tokens.append(push_tokens(k))

    seg_p.wait_recv()
    seg_f.wait_recv()
    for kb in range(4):
        key_seg = seg[kb].astype(F32)
        if kb < 2:
            key_seg = jnp.where(z == 0, -1.0, key_seg)
        key_seg = jnp.broadcast_to(key_seg, (128, 128)).T
        for qb in range(2):
            query_seg = jnp.broadcast_to(seg[2 + qb].astype(F32), (128, 128))
            j = kb * 128 + lax.broadcasted_iota(jnp.int32, (128, 128), 0)
            i = (2 + qb) * 128 + lax.broadcasted_iota(jnp.int32, (128, 128), 1)
            allowed = (j <= i) & (key_seg == query_seg)
            bias[kb * 128:(kb + 1) * 128, qb * 128:(qb + 1) * 128] = jnp.where(allowed, 0.0, -1e30)

    l_lat[0].wait()
    lat_p.wait_recv()
    lat_f.wait_recv()
    r = lax.broadcasted_iota(jnp.int32, (512, 512), 0)
    source = 32 * (4 * ((r >> 3) & 3) + ((r >> 5) & 3)) + 16 * ((r >> 2) & 1) + 4 * (r >> 7) + (r & 3)
    to_owner = jnp.where(lax.broadcasted_iota(jnp.int32, (512, 512), 1) == source, 1.0, 0.0).astype(BF16)
    ctp[...] = mm_nt(to_owner, lat[:, :512]).astype(BF16)
    e_row = lax.broadcasted_iota(jnp.int32, (64, 128), 0)
    e_col = lax.broadcasted_iota(jnp.int32, (64, 128), 1)
    rope_keys = lat[:, 512:576]
    rope0[...] = mm(rope_keys, jnp.where(e_col == e_row, 1.0, 0.0).astype(BF16)).astype(BF16)
    rope1[...] = mm(rope_keys, jnp.where(e_col == e_row + 64, 1.0, 0.0).astype(BF16))
    lacc[...] = jnp.zeros_like(lacc)
    racc[...] = jnp.zeros_like(racc)
    low_half = lax.broadcasted_iota(jnp.int32, (512, 128), 1) < 64

    def compute(k, between):
        p = order[k]
        for copy in l_w[k] + l_q[k]:
            copy.wait()
        for copy in tokens[k]:
            copy.wait_recv()
        keys = mm(lat[:, :512], wk[p])
        turned = pltpu.roll(keys[:, 128:], 64, 1)
        kx[0, :, :128] = keys[:, :128].astype(BF16)
        kx[0, :, 128:] = rope0[...]
        kx[1, :, :128] = jnp.where(low_half, 0.0, turned).astype(BF16)
        kx[1, :, 128:] = jnp.where(low_half, turned, rope1[...]).astype(BF16)
        vx[...] = mm(lat[:, :512], wv[p]).astype(BF16)
        dqs = []
        for h in range(2):
            qx = qs[p, :, 128 * h:128 * h + 256]
            gh = gs[p, :, 128 * h:128 * h + 128]
            scores = mm_nt(kx[h], qx) + bias[...]
            top = jnp.max(scores, axis=0, keepdims=True)
            numer = jnp.exp((scores - top) * SCALE)
            weights = numer * (1.0 / jnp.sum(numer, axis=0, keepdims=True))
            low = weights.astype(BF16)
            prob_grad = mm_nt(vx[:, 128 * h:128 * h + 128], gh)
            out_dot = jnp.sum(low.astype(F32) * prob_grad, axis=0, keepdims=True)
            score_grad = (SCALE * weights * (prob_grad - out_dot)).astype(BF16)
            dvp[:, 128 * h:128 * h + 128] = mm(low, gh).astype(BF16)
            dkx = mm(score_grad, qx)
            if h == 0:
                dkp[:, :128] = dkx[:, :128].astype(BF16)
                racc[...] += dkx[:, 128:]
            else:
                t0 = pltpu.roll(dkx[:, :128], 64, 1)
                t1 = pltpu.roll(dkx[:, 128:], 64, 1)
                dkp[:, 128:] = jnp.where(low_half, t0, t1).astype(BF16)
                racc[...] += t1
            dqs.append(mm_tn(score_grad, kx[h]))
            if h == 0:
                between()
        dq[p, :, :128] = dqs[0][:, :128].astype(BF16)
        dq[p, :, 128:256] = (dqs[0][:, 128:] + dqs[1][:, :128]).astype(BF16)
        dq[p, :, 256:] = dqs[1][:, 128:].astype(BF16)
        u[p] = mm(ctp[...], dkp[...]).astype(BF16)
        lacc[...] += mm_nt(dkp[...], wk[p]) + mm_nt(dvp[...], wv[p])

    def push_queries(k):
        p = order[k]
        where = cols(c * 1536 + p * 384, 384)
        moved = push(dq.at[p, rows(oc * 128, 128)], qg_out.at[:, where], pair)
        return moved, local(dq.at[p, rows(c * 128, 128)], qg_out.at[:, where])

    def step1(k):
        p = order[k]
        return (
            push(u.at[p, rows(far * 128, 128), pl.ds(0, 128)], ra.at[p], at(x_to=right)),
            push(u.at[p, rows(far * 128, 128), pl.ds(128, 128)], rb.at[p], at(x_to=left)),
            push(u.at[p, rows(right * 128, 128), pl.ds(128, 128)], rlb.at[p], at(x_to=right)),
            push(u.at[p, rows(left * 128, 128), pl.ds(0, 128)], rra.at[p], at(x_to=left)),
        )

    def step2(k, first):
        p = order[k]
        first[0].wait_recv()
        sa[p] = (u[p, rows(right * 128, 128), :128].astype(F32) + ra[p].astype(F32)).astype(BF16)
        to_right = push(sa.at[p], rla.at[p], at(x_to=right))
        first[1].wait_recv()
        sb[p] = (u[p, rows(left * 128, 128), 128:].astype(F32) + rb[p].astype(F32)).astype(BF16)
        return to_right, push(sb.at[p], rrb.at[p], at(x_to=left))

    def step3(k, first, second):
        p = order[k]
        for copy in (first[2], first[3], second[0], second[1]):
            copy.wait_recv()
        mine = u[p, rows(x * 128, 128), :].astype(F32)
        a = mine[:, :128] + rla[p].astype(F32) + rra[p].astype(F32)
        b = mine[:, 128:] + rlb[p].astype(F32) + rrb[p].astype(F32)
        tb[p, :, :128] = a.astype(BF16)
        tb[p, :, 128:] = b.astype(BF16)
        out = []
        for i, d in enumerate((-1, 1, 2)):
            part = tb.at[p, rows(((z + d + 4) % 4) * 32, 32)]
            out.append(push(part, za.at[i, p], at(dz=d)))
        return out

    for copy in xf0:
        copy.wait_recv()
    zf0 = forward_z(0)
    xf1 = []
    queries = []
    compute(0, lambda: xf1.extend(forward_x(1)))
    queries.append(push_queries(0))
    a0 = step1(0)
    for copy in xf1:
        copy.wait_recv()
    zf1 = forward_z(1)
    compute(1, lambda: None)
    queries.append(push_queries(1))
    a1 = step1(1)
    b0 = step2(0, a0)
    for copy in zf0:
        copy.wait_recv()
    compute(2, lambda: None)
    queries.append(push_queries(2))
    a2 = step1(2)
    b1 = step2(1, a1)
    c0 = step3(0, a0, b0)
    for copy in zf1:
        copy.wait_recv()
    compute(3, lambda: None)
    a3 = step1(3)
    for block in range(4):
        at_rows = slice(block * 128, block * 128 + 128)
        lb[block, :, :512] = lacc[at_rows, :].astype(BF16)
        lb[block, :, 512:576] = racc[at_rows, :64].astype(BF16)
    h1 = push(lb.at[oc], p1.at[0], pair), push(lb.at[2 + oc], p1.at[1], pair)
    queries.append(push_queries(3))
    b2 = step2(2, a2)
    c1 = step3(1, a1, b1)
    b3 = step2(3, a3)
    h2 = []
    for i in range(2):
        h1[i].wait_recv()
        l2[i] = (lb[2 * i + c].astype(F32) + p1[i].astype(F32)).astype(BF16)
        for dy in range(4):
            yt = (y + dy) % 4
            if i == 1 and dy == 0:
                continue
            h2.append(push(l2.at[i, rows(yt * 32, 32)], p2.at[i * 4 + dy], at(dz=i - 1, y_to=yt)))
    c2 = step3(2, a2, b2)
    c3 = step3(3, a3, b3)
    for copy in h2:
        copy.wait_recv()
    total = l2[1, rows(y * 32, 32), :].astype(F32)
    for i in (0, 1, 2, 3, 5, 6, 7):
        total = total + p2[i].astype(F32)
    fl[...] = total.astype(BF16)
    h3 = [push(fl, lg_out.at[rows(y * 32, 32)], at(y_to=(y + dy) % 4)) for dy in (1, 2, 3)]
    l_fl = local(fl, lg_out.at[rows(y * 32, 32)])

    stacked = []
    for p in range(4):
        stacked.append(tb[p, rows((z % 4) * 32, 32), :].astype(F32))
    for copies in (c0, c1, c2, c3):
        for copy in copies:
            copy.wait_recv()
    for p in range(4):
        for i in range(3):
            stacked[p] = stacked[p] + za[i, p].astype(F32)
    stacked = jnp.concatenate(stacked, axis=0).astype(BF16)
    r = lax.broadcasted_iota(jnp.int32, (128, 128), 0)
    source = ((r >> 2) & 3) * 32 + (r >> 4) * 4 + (r & 3)
    regroup = jnp.where(lax.broadcasted_iota(jnp.int32, (128, 128), 1) == source, 1.0, 0.0).astype(BF16)
    regrouped = mm(regroup, stacked).astype(BF16)
    for i in range(8):
        zp[i] = regrouped[16 * i:16 * i + 16]
    h4 = []
    for da in range(4):
        for dc in range(2):
            if da == 0 and dc == 0:
                continue
            core = c if dc == 0 else oc
            piece = (z // 4 + da) % 4 * 2 + core
            h4.append(push(zp.at[piece], zb.at[da * 2 + dc], at(dz=4 * da, core=core)))
    for copy in h4:
        copy.wait_recv()
    for dc in range(2):
        mine = zp[z // 4 * 2 + c] if dc == 0 else zb[dc]
        total = mine.astype(F32)
        for da in (1, 2, 3):
            total = total + zb[da * 2 + dc].astype(F32)
        base = (c if dc == 0 else oc) * 1024
        for p in range(4):
            ku_out[:, cols(base + p * 256, 256)] = total[4 * p:4 * p + 4, :]
    for copy in h3:
        copy.wait_recv()
    l_fl.wait()
    for moved, kept in queries:
        moved.wait_recv()
        kept.wait()
    for copy in sends:
        copy.wait_send()


def local_part(latent, queries, out_grad, segment_ids, key_up, value_up):
    hbm = pl.BlockSpec(memory_space=pl.ANY)
    vmem = pl.BlockSpec(memory_space=pltpu.VMEM)
    V = pltpu.VMEM
    outs = pl.pallas_call(
        kernel,
        out_shape=(
            jax.ShapeDtypeStruct((128, 3072), BF16),
            jax.ShapeDtypeStruct((128, 576), BF16),
            jax.ShapeDtypeStruct((4, 2048), F32),
        ),
        in_specs=[hbm, hbm, hbm, vmem, hbm, hbm],
        out_specs=[hbm, hbm, vmem],
        scratch_shapes=[
            V((4, 512, 256), BF16), V((4, 512, 256), BF16),
            V((4, 256, 384), BF16), V((4, 256, 256), BF16),
            V((512, 576), BF16), V((4, 1, 128), jnp.int32),
            V((512, 256), F32), V((512, 512), BF16),
            V((512, 128), BF16), V((512, 128), F32),
            V((2, 512, 256), BF16), V((512, 256), BF16),
            V((4, 256, 384), BF16), V((4, 512, 256), BF16),
            V((512, 512), F32), V((512, 128), F32),
            V((512, 256), BF16), V((512, 256), BF16),
            V((4, 128, 128), BF16), V((4, 128, 128), BF16),
            V((4, 128, 128), BF16), V((4, 128, 128), BF16),
            V((4, 128, 128), BF16), V((4, 128, 128), BF16),
            V((4, 128, 128), BF16), V((4, 128, 128), BF16),
            V((4, 128, 256), BF16), V((3, 4, 32, 256), BF16),
            V((8, 16, 256), BF16), V((8, 16, 256), BF16),
            V((4, 128, 576), BF16), V((2, 128, 576), BF16),
            V((2, 128, 576), BF16), V((8, 32, 576), BF16),
            V((32, 576), BF16),
            pltpu.SemaphoreType.DMA((N_REMOTE,)),
            pltpu.SemaphoreType.DMA((N_REMOTE,)),
            pltpu.SemaphoreType.DMA((N_LOCAL,)),
        ],
        compiler_params=pltpu.CompilerParams(
            collective_id=0, has_side_effects=True, vmem_limit_bytes=50 * 1024 * 1024
        ),
    )(latent[0], queries[0], out_grad[0], segment_ids, key_up, value_up)
    return outs[0][None], outs[1][None], outs[2]


def solution(mesh):
    return jax.shard_map(
        local_part,
        mesh=mesh,
        in_specs=(
            P("dp", "ctx", None),
            P("dp", "ctx", "head"),
            P("dp", "ctx", "head"),
            P("dp", "ctx"),
            P("dp", "head"),
            P("dp", "head"),
        ),
        out_specs=(P("dp", "ctx", "head"), P("dp", "ctx", None), P(("ctx", "dp"), "head")),
        check_vma=False,
    )
```

time: 488 us -> 72.2 us (0.15)
  waiting for transfers between devices: 386 us -> 0 us
  Pallas kernels: 0 us -> 62.9 us
  matrix products: 32.5 us -> 0 us
  blocking collectives: 18.2 us -> 0 us
  starting transfers between devices: 18.2 us -> 0 us
  between operations: 14.8 us -> 0.65 us
  local copies, waits for them, and re-layouts: 13.8 us -> 8.25 us
    unnamed x4 -> x0, waiting for transfers between devices: 321 us -> none
    pallas_call x0 -> x1, Pallas kernels: none -> 62.9 us  [local_part(): pl.pallas_call(kernel, out_shape=(jax.ShapeDtypeStruct((128, 3072), BF16)...]
    all_gather x2 -> x0, waiting for transfers between devices: 60.5 us -> none  [the longest x1 34.4 us: local(): lax.all_gather(key_up, 'dp', axis=0, tiled=True)]
    dot_general x14 -> x0, matrix products: 32.5 us -> none  [the longest x1 5.3 us: attend(): jnp.einsum('hij,ihd->jhd', weights_low, grad_block, preferred_element_typ...]
    psum x1 -> x0, blocking collectives: 18.2 us -> none  [local(): total_grad = lax.psum(total_grad, 'head')]
    ppermute x6 -> x0, starting transfers between devices: 18.1 us -> none  [shifted(): return lax.ppermute(x, axis, pairs)]
  transfers between devices with their start and end apart: 9 -> 0, of which waited for: 5 -> 0; matrix products, arithmetic and copies ran while one was open for 4% -> 0% of each run, Pallas kernels for 0% -> 0%
where the time goes in v1:
time: 72.2 us; the launch traced here: 71.8 us
  Pallas kernels  62.9 us (87%)
  local copies, waits for them, and re-layouts  8.25 us (11%)
    pallas_call x1, Pallas kernels, local_part(): pl.pallas_call(kernel, out_shape=(jax.ShapeDtypeStruct((128, 3072), BF16)...  62.9 us
    unnamed x14, local copies, waits for them, and re-layouts  8.25 us

profile of v1, /device:TPU:1, one launch (start us, length us, event | category | flops | bytes accessed | tf_op | source)
XLA Modules:
  0.0 71.8 jit_solution(14254629165016842903)
XLA Ops:
  0.6 1.1 %copy.9 = bf16[1,128,576]{2,1,0:T(8,128)(2,1)S(1)} copy(bf16[1,128,576]{1,2,0:T(8,128)(2,1)} %param.6) | data formatting | bytes 294912 | tf_op args[0]
  1.7 0.0 copy-start.4
  1.7 0.6 copy-done.4
  2.4 0.0 copy-start
  2.4 1.1 %copy-done = bf16[1,128,3072]{2,1,0:T(8,128)(2,1)S(1)} copy-done((bf16[1,128,3072]{2,1,0:T(8,128)(2,1)S(1)}, bf16[1,128,3072]{2,1,0:T(8,128)(2,1)}, u32[]{:S(2)}) %copy-start) | copy-done | bytes 786456
  3.5 0.0 copy-start.1
  3.5 1.0 %copy-done.1 = bf16[1,128,2048]{2,1,0:T(8,128)(2,1)S(1)} copy-done((bf16[1,128,2048]{2,1,0:T(8,128)(2,1)S(1)}, bf16[1,128,2048]{2,1,0:T(8,128)(2,1)}, u32[]{:S(2)}) %copy-start.1) | copy-done | bytes 524312
  4.5 0.0 copy-start.2
  4.5 1.0 %copy-done.2 = bf16[128,2048]{1,0:T(8,128)(2,1)S(1)} copy-done((bf16[128,2048]{1,0:T(8,128)(2,1)S(1)}, bf16[128,2048]{1,0:T(8,128)(2,1)}, u32[]{:S(2)}) %copy-start.2) | copy-done | bytes 524312
  5.6 0.0 copy-start.3
  5.6 1.0 %copy-done.3 = bf16[128,2048]{1,0:T(8,128)(2,1)S(1)} copy-done((bf16[128,2048]{1,0:T(8,128)(2,1)S(1)}, bf16[128,2048]{1,0:T(8,128)(2,1)}, u32[]{:S(2)}) %copy-start.3) | copy-done | bytes 524312
  6.6 62.9 %shard_map.85 = (bf16[128,3072]{1,0:T(8,128)(2,1)S(1)}, bf16[128,576]{1,0:T(8,128)(2,1)S(1)}, f32[4,2048]{1,0:T(4,128)S(1)}) custom-call(bf16[128,576]{1,0:T(8,128)(2,1)S(1)} %bitcast.7, bf16[128,3072]{1,0:T(8,128)(2,1)S(1)} %bitcast.6, bf16[128,2048]{1,0:T(8,128)(2,1)S(1)} %bitcast.8, s32[1,128]{1,0:T(1,128)S(1)} %copy-done.4, ...), custom_call_target="tpu_custom_call" | custom-call | tf_op jit(solution)/shard_map/pallas_call | solution.py:378
  69.6 0.8 %copy.10 = bf16[1,128,576]{1,2,0:T(8,128)(2,1)} copy(bf16[1,128,576]{2,1,0:T(8,128)(2,1)S(1)} %bitcast.9) | data formatting | bytes 294912
  70.4 0.9 %copy.13 = bf16[1,128,3072]{2,1,0:T(8,128)(2,1)} copy(bf16[1,128,3072]{2,1,0:T(8,128)(2,1)S(1)} %bitcast.5) | data formatting | bytes 1572864
  71.2 0.6 copy.14
Async XLA Ops:
  1.7 0.7 copy-start.4
  2.4 1.1 %copy-start = (bf16[1,128,3072]{2,1,0:T(8,128)(2,1)S(1)}, bf16[1,128,3072]{2,1,0:T(8,128)(2,1)}, u32[]{:S(2)}) copy-start(bf16[1,128,3072]{2,1,0:T(8,128)(2,1)} %param.7) | copy-start | bytes 2359300
  3.5 1.0 %copy-start.1 = (bf16[1,128,2048]{2,1,0:T(8,128)(2,1)S(1)}, bf16[1,128,2048]{2,1,0:T(8,128)(2,1)}, u32[]{:S(2)}) copy-start(bf16[1,128,2048]{2,1,0:T(8,128)(2,1)} %param.8) | copy-start | bytes 1572868
  4.5 1.0 %copy-start.2 = (bf16[128,2048]{1,0:T(8,128)(2,1)S(1)}, bf16[128,2048]{1,0:T(8,128)(2,1)}, u32[]{:S(2)}) copy-start(bf16[128,2048]{1,0:T(8,128)(2,1)} %wk_in.1) | copy-start | bytes 1572868
  5.6 1.0 %copy-start.3 = (bf16[128,2048]{1,0:T(8,128)(2,1)S(1)}, bf16[128,2048]{1,0:T(8,128)(2,1)}, u32[]{:S(2)}) copy-start(bf16[128,2048]{1,0:T(8,128)(2,1)} %wv_in.1) | copy-start | bytes 1572868

commit v2 on v1

v2 whole, which is shorter than its diff:
```python
import jax
import jax.numpy as jnp
from jax import lax
from jax.experimental import pallas as pl
from jax.experimental.pallas import tpu as pltpu
from jax.sharding import PartitionSpec as P

F32 = jnp.float32
BF16 = jnp.bfloat16
SCALE = (128 + 64) ** -0.5
N_REMOTE = 160
N_LOCAL = 40


def mm(a, b):
    return lax.dot_general(a, b, (((1,), (0,)), ((), ())), preferred_element_type=F32)


def mm_nt(a, b):
    return lax.dot_general(a, b, (((1,), (1,)), ((), ())), preferred_element_type=F32)


def mm_tn(a, b):
    return lax.dot_general(a, b, (((0,), (0,)), ((), ())), preferred_element_type=F32)


def rows(start, size):
    return pl.ds(pl.multiple_of(start, size), size)


def cols(start, size):
    return pl.ds(pl.multiple_of(start, 128), size)


def kernel(
    lat_in, qry_in, grd_in, seg_in, wk_in, wv_in,
    qg_out, lg_out, ku_out,
    wk, wv, qs, gs, latt, lat, seg, bias, ctp, to_owner, rope0, rope1, kx, vx, dq, u, lacc, racc, dkp, dvp,
    ux, tz, zr, ksum, kpeer, lb, p1, l2, p2, fl,
    send_sem, recv_sem, local_sem,
):
    s = lax.axis_index("ctx")
    y = lax.axis_index("head")
    x = lax.axis_index("dp")
    z = s // 2
    c = s % 2
    oc = 1 - c
    par = z % 2
    n_z = lax.axis_size("ctx") // 2
    order = [par, 2 + par, 1 - par, 3 - par]

    def at(dz=0, core=None, x_to=None, y_to=None):
        core = c if core is None else core
        zt = (z + dz + n_z) % n_z
        return {
            "ctx": zt * 2 + core,
            "head": y if y_to is None else y_to,
            "dp": x if x_to is None else x_to,
        }

    right, left, far = (x + 1) % 4, (x + 3) % 4, (x + 2) % 4
    pair = at(core=oc)
    sends = []
    locals_ = []
    count = [0, 0]

    def push(src, dst, dev):
        i = count[0]
        count[0] += 1
        copy = pltpu.make_async_remote_copy(
            src_ref=src, dst_ref=dst, send_sem=send_sem.at[i], recv_sem=recv_sem.at[i],
            device_id=dev, device_id_type=pl.DeviceIdType.MESH,
        )
        copy.start()
        sends.append(copy)
        return copy

    def local(src, dst):
        i = count[1]
        count[1] += 1
        copy = pltpu.make_async_copy(src, dst, local_sem.at[i])
        copy.start()
        return copy

    partners = [pair, at(x_to=right), at(x_to=left), at(x_to=far)]
    partners += [at(dz=d) for d in range(1, 16)]
    for dy in (1, 2, 3):
        yt = (y + dy) % 4
        partners += [at(y_to=yt), at(dz=-1, y_to=yt), at(dz=1, y_to=yt)]
    barrier = pltpu.get_barrier_semaphore()
    for dev in partners:
        pl.semaphore_signal(barrier, inc=1, device_id=dev, device_id_type=pl.DeviceIdType.MESH)

    l_lat = local(lat_in, latt.at[2 + c])
    l_seg = local(seg_in, seg.at[2 + c])
    l_w, l_q = [], []
    for p in order:
        l_w.append((
            local(wk_in.at[:, cols(c * 1024 + p * 256, 256)], wk.at[p, rows(x * 128, 128)]),
            local(wv_in.at[:, cols(c * 1024 + p * 256, 256)], wv.at[p, rows(x * 128, 128)]),
        ))
        l_q.append((
            local(qry_in.at[:, cols(c * 1536 + p * 384, 384)], qs.at[p, rows(c * 128, 128)]),
            local(grd_in.at[:, cols(c * 1024 + p * 256, 256)], gs.at[p, rows(c * 128, 128)]),
        ))

    r = lax.broadcasted_iota(jnp.int32, (512, 512), 0)
    source = 32 * ((r >> 3) & 15) + 16 * ((r >> 2) & 1) + 4 * (r >> 7) + (r & 3)
    to_owner[...] = jnp.where(lax.broadcasted_iota(jnp.int32, (512, 512), 1) == source, 1.0, 0.0).astype(BF16)
    lacc[...] = jnp.zeros_like(lacc)
    racc[...] = jnp.zeros_like(racc)
    pl.semaphore_wait(barrier, len(partners))

    def push_direct(k):
        p = order[k]
        out = []
        for w_in, w in ((wk_in, wk), (wv_in, wv)):
            src = w_in.at[:, cols(c * 1024 + p * 256, 256)]
            out.append([
                push(src, w.at[p, rows(x * 128, 128)], at(x_to=x_to)) for x_to in (far, right, left)
            ])
        return out

    lat_z = push(lat_in, latt.at[c], at(dz=1))
    seg_z = push(seg_in, seg.at[c], at(dz=1))
    direct = [push_direct(0)]
    lat_p = push(lat_in, latt.at[2 + c], pair)
    seg_p = push(seg_in, seg.at[2 + c], pair)

    def push_tokens(k):
        p = order[k]
        return (
            push(qry_in.at[:, cols(oc * 1536 + p * 384, 384)], qs.at[p, rows(c * 128, 128)], pair),
            push(grd_in.at[:, cols(oc * 1024 + p * 256, 256)], gs.at[p, rows(c * 128, 128)], pair),
        )

    tokens = [push_tokens(0)]

    def forward_z(k, part):
        p = order[k]
        w = (wk, wv)[part]
        for copy in direct[k][part]:
            copy.wait_recv()
        out = []
        for start, size, dz in (
            (right * 128, 128, 1), (left * 128, 128, -1), (far * 128, 64, 1), (far * 128 + 64, 64, -1),
        ):
            piece = w.at[p, rows(start, size)]
            out.append(push(piece, piece, at(dz=dz)))
        return out

    lat_z.wait_recv()
    lat_f = push(latt.at[c], latt.at[c], pair)
    seg_z.wait_recv()
    seg_f = push(seg.at[c], seg.at[c], pair)
    direct.append(push_direct(1))
    for k in (1, 2, 3):
        tokens.append(push_tokens(k))

    zf = {(0, 0): forward_z(0, 0)}

    l_seg.wait()
    seg_p.wait_recv()
    seg_f.wait_recv()
    for kb in range(4):
        key_seg = seg[kb].astype(F32)
        if kb < 2:
            key_seg = jnp.where(z == 0, -1.0, key_seg)
        key_seg = jnp.broadcast_to(key_seg, (128, 128)).T
        for qb in range(2):
            query_seg = jnp.broadcast_to(seg[2 + qb].astype(F32), (128, 128))
            j = kb * 128 + lax.broadcasted_iota(jnp.int32, (128, 128), 0)
            i = (2 + qb) * 128 + lax.broadcasted_iota(jnp.int32, (128, 128), 1)
            allowed = (j <= i) & (key_seg == query_seg)
            bias[kb * 128:(kb + 1) * 128, qb * 128:(qb + 1) * 128] = jnp.where(allowed, 0.0, -1e30)

    l_lat.wait()
    lat_p.wait_recv()
    lat_f.wait_recv()
    for block in range(4):
        at_rows = slice(block * 128, block * 128 + 128)
        ctp[:, at_rows] = mm(to_owner[...], latt[block, :512, :]).astype(BF16)
        lat[at_rows, :] = latt[block].T
    e_row = lax.broadcasted_iota(jnp.int32, (64, 128), 0)
    e_col = lax.broadcasted_iota(jnp.int32, (64, 128), 1)
    rope_keys = lat[:, 512:576]
    rope0[...] = mm(rope_keys, jnp.where(e_col == e_row, 1.0, 0.0).astype(BF16)).astype(BF16)
    rope1[...] = mm(rope_keys, jnp.where(e_col == e_row + 64, 1.0, 0.0).astype(BF16))
    low_half = lax.broadcasted_iota(jnp.int32, (512, 128), 1) < 64

    def compute(k, mid, after, finish=lambda: None):
        p = order[k]
        for copy in l_w[k] + l_q[k]:
            copy.wait()
        for copy in tokens[k]:
            copy.wait_recv()
        keys = mm(lat[:, :512], wk[p])
        turned = pltpu.roll(keys[:, 128:], 64, 1)
        kx[0, :, :128] = keys[:, :128].astype(BF16)
        kx[0, :, 128:] = rope0[...]
        kx[1, :, :128] = jnp.where(low_half, 0.0, turned).astype(BF16)
        kx[1, :, 128:] = jnp.where(low_half, turned, rope1[...]).astype(BF16)
        vx[...] = mm(lat[:, :512], wv[p]).astype(BF16)
        grads = []
        for h in range(2):
            qx = qs[p, :, 128 * h:128 * h + 256]
            gh = gs[p, :, 128 * h:128 * h + 128]
            scores = mm_nt(kx[h], qx) + bias[...]
            top = jnp.max(scores, axis=0, keepdims=True)
            numer = jnp.exp((scores - top) * SCALE)
            weights = numer * (1.0 / jnp.sum(numer, axis=0, keepdims=True))
            low = weights.astype(BF16)
            prob_grad = mm_nt(vx[:, 128 * h:128 * h + 128], gh)
            out_dot = jnp.sum(low.astype(F32) * prob_grad, axis=0, keepdims=True)
            score_grad = (SCALE * weights * (prob_grad - out_dot)).astype(BF16)
            dkx = mm(score_grad, qx)
            if h == 0:
                dkp[:, :128] = dkx[:, :128].astype(BF16)
                racc[...] += dkx[:, 128:]
                mid()
            else:
                t0 = pltpu.roll(dkx[:, :128], 64, 1)
                t1 = pltpu.roll(dkx[:, 128:], 64, 1)
                dkp[:, 128:] = jnp.where(low_half, t0, t1).astype(BF16)
                racc[...] += t1
            grads.append((low, gh, score_grad))
        u[p] = mm(ctp[...], dkp[...]).astype(BF16)
        after()
        dqs = []
        for h, (low, gh, score_grad) in enumerate(grads):
            dvp[:, 128 * h:128 * h + 128] = mm(low, gh).astype(BF16)
            dqs.append(mm_tn(score_grad, kx[h]))
        lacc[...] += mm_nt(dkp[...], wk[p]) + mm_nt(dvp[...], wv[p])
        finish()
        dq[p, :, :128] = dqs[0][:, :128].astype(BF16)
        dq[p, :, 128:256] = (dqs[0][:, 128:] + dqs[1][:, :128]).astype(BF16)
        dq[p, :, 256:] = dqs[1][:, 128:].astype(BF16)

    def push_queries(k):
        p = order[k]
        where = cols(c * 1536 + p * 384, 384)
        moved = push(dq.at[p, rows(oc * 128, 128)], qg_out.at[:, where], pair)
        return moved, local(dq.at[p, rows(c * 128, 128)], qg_out.at[:, where])

    def push_x(k):
        p = order[k]
        return [
            push(u.at[p, rows(x_to * 128, 128)], ux.at[i, p], at(x_to=x_to))
            for i, x_to in enumerate((far, right, left))
        ]

    def sum_x(i, arriving):
        p = order[turns[i]]
        for copy in arriving:
            copy.wait_recv()
        total = u[p, rows(x * 128, 128), :].astype(F32)
        for j in range(3):
            total = total + ux[j, p].astype(F32)
        total = total.reshape(16, 8, 256)
        tz[:, i] = jnp.concatenate([total[:, :, :128], total[:, :, 128:]], axis=1).astype(BF16)

    def push_z(first, size):
        out = []
        for d in (8, 7, 9, 6, 10, 5, 11, 4, 12, 3, 13, 2, 14, 1, 15):
            src = tz.at[(z + d) % 16, pl.ds(first, size)]
            out.append(push(src, zr.at[d, pl.ds(first, size)], at(dz=d)))
        return out

    turns = (0, 2, 1, 3)
    queries = []
    over_x = []
    over_z = []
    zf[0, 1] = forward_z(0, 1)

    def pushed_x(k):
        return lambda: over_x.append(push_x(k))

    compute(0, lambda: None, pushed_x(0))
    zf[1, 0] = forward_z(1, 0)
    queries.append(push_queries(0))
    for part in range(2):
        for copy in zf[0, part]:
            copy.wait_recv()
    compute(2, lambda: zf.update({(1, 1): forward_z(1, 1)}), pushed_x(2))
    queries.append(push_queries(2))

    def next_z(i):
        sum_x(i, over_x[i])
        over_z.extend(push_z(i, 1))

    compute(1, lambda: next_z(0), pushed_x(1))
    queries.append(push_queries(1))
    next_z(1)
    for part in range(2):
        for copy in zf[1, part]:
            copy.wait_recv()
    h1 = []

    def start_latent():
        for block in range(4):
            at_rows = slice(block * 128, block * 128 + 128)
            lb[block, :, :512] = lacc[at_rows, :].astype(BF16)
            lb[block, :, 512:576] = racc[at_rows, :64].astype(BF16)
        h1.append(push(lb.at[oc], p1.at[0], pair))
        h1.append(push(lb.at[2 + oc], p1.at[1], pair))

    compute(3, lambda: next_z(2), pushed_x(3), start_latent)
    queries.append(push_queries(3))
    h2 = []
    for i in range(2):
        h1[i].wait_recv()
        l2[i] = (lb[2 * i + c].astype(F32) + p1[i].astype(F32)).astype(BF16)
        for dy in range(4):
            yt = (y + dy) % 4
            if i == 1 and dy == 0:
                continue
            h2.append(push(l2.at[i, rows(yt * 32, 32)], p2.at[i * 4 + dy], at(dz=i - 1, y_to=yt)))
    next_z(3)
    for copy in h2:
        copy.wait_recv()
    total = l2[1, rows(y * 32, 32), :].astype(F32)
    for i in (0, 1, 2, 3, 5, 6, 7):
        total = total + p2[i].astype(F32)
    fl[...] = total.astype(BF16)
    h3 = [push(fl, lg_out.at[rows(y * 32, 32)], at(y_to=(y + dy) % 4)) for dy in (1, 2, 3)]
    l_fl = local(fl, lg_out.at[rows(y * 32, 32)])

    for copy in over_z:
        copy.wait_recv()
    for k in range(4):
        i = turns.index(k)
        other = turns.index((k + 2) % 4)
        total = tz[z, i].astype(F32)
        for d in range(1, 16):
            total = total + zr[d, i if d % 2 == 0 else other].astype(F32)
        ksum[:, cols(order[k] * 256, 128)] = total[:8]
        ksum[:, cols(order[k] * 256 + 128, 128)] = total[8:]
    swap = push(ksum, kpeer, pair)
    ku_out[:, cols(c * 1024, 1024)] = jnp.where(c == 0, ksum[:4, :], ksum[4:, :])
    swap.wait_recv()
    ku_out[:, cols(oc * 1024, 1024)] = jnp.where(c == 0, kpeer[:4, :], kpeer[4:, :])
    for copy in h3:
        copy.wait_recv()
    l_fl.wait()
    for moved, kept in queries:
        moved.wait_recv()
        kept.wait()
    for copy in sends:
        copy.wait_send()


def local_part(latent, queries, out_grad, segment_ids, key_up, value_up):
    hbm = pl.BlockSpec(memory_space=pl.ANY)
    vmem = pl.BlockSpec(memory_space=pltpu.VMEM)
    V = pltpu.VMEM
    outs = pl.pallas_call(
        kernel,
        out_shape=(
            jax.ShapeDtypeStruct((128, 3072), BF16),
            jax.ShapeDtypeStruct((128, 576), BF16),
            jax.ShapeDtypeStruct((4, 2048), F32),
        ),
        in_specs=[hbm] * 6,
        out_specs=[hbm, hbm, vmem],
        scratch_shapes=[
            V((4, 512, 256), BF16), V((4, 512, 256), BF16),
            V((4, 256, 384), BF16), V((4, 256, 256), BF16),
            V((4, 576, 128), BF16), V((512, 576), BF16), V((4, 1, 128), jnp.int32),
            V((512, 256), F32), V((512, 512), BF16), V((512, 512), BF16),
            V((512, 128), BF16), V((512, 128), F32),
            V((2, 512, 256), BF16), V((512, 256), BF16),
            V((4, 256, 384), BF16), V((4, 512, 256), BF16),
            V((512, 512), F32), V((512, 128), F32),
            V((512, 256), BF16), V((512, 256), BF16),
            V((3, 4, 128, 256), BF16),
            V((16, 4, 16, 128), BF16), V((16, 4, 16, 128), BF16),
            V((8, 1024), F32), V((8, 1024), F32),
            V((4, 128, 576), BF16), V((2, 128, 576), BF16),
            V((2, 128, 576), BF16), V((8, 32, 576), BF16),
            V((32, 576), BF16),
            pltpu.SemaphoreType.DMA((N_REMOTE,)),
            pltpu.SemaphoreType.DMA((N_REMOTE,)),
            pltpu.SemaphoreType.DMA((N_LOCAL,)),
        ],
        compiler_params=pltpu.CompilerParams(
            collective_id=0, has_side_effects=True, vmem_limit_bytes=60 * 1024 * 1024
        ),
    )(latent[0].T, queries[0], out_grad[0], segment_ids, key_up, value_up)
    return outs[0][None], outs[1][None], outs[2]


def solution(mesh):
    return jax.shard_map(
        local_part,
        mesh=mesh,
        in_specs=(
            P("dp", "ctx", None),
            P("dp", "ctx", "head"),
            P("dp", "ctx", "head"),
            P("dp", "ctx"),
            P("dp", "head"),
            P("dp", "head"),
        ),
        out_specs=(P("dp", "ctx", "head"), P("dp", "ctx", None), P(("ctx", "dp"), "head")),
        check_vma=False,
    )
```

time: 72.2 us -> 64.6 us (0.89)
  local copies, waits for them, and re-layouts: 8.25 us -> 4.38 us
  Pallas kernels: 62.9 us -> 59.5 us
    unnamed x14 -> x5, local copies, waits for them, and re-layouts: 8.25 us -> 4.38 us
    pallas_call x1, Pallas kernels: 62.9 us -> 59.5 us  [local_part(): pl.pallas_call(kernel, out_shape=(jax.ShapeDtypeStruct((128, 3072), BF16)...]
where the time goes in v2:
time: 64.6 us; the launch traced here: 64.5 us
  Pallas kernels  59.5 us (92%)
  local copies, waits for them, and re-layouts  4.38 us (7%)
    pallas_call x1, Pallas kernels, local_part(): pl.pallas_call(kernel, out_shape=(jax.ShapeDtypeStruct((128, 3072), BF16)...  59.5 us
    unnamed x5, local copies, waits for them, and re-layouts  4.38 us

profile of v2, /device:TPU:1, one launch (start us, length us, event | category | flops | bytes accessed | tf_op | source)
XLA Modules:
  0.0 64.5 jit_solution(5813721418916808267)
XLA Ops:
  0.6 59.5 %shard_map.85 = (bf16[128,3072]{1,0:T(8,128)(2,1)}, bf16[128,576]{1,0:T(8,128)(2,1)}, f32[4,2048]{1,0:T(4,128)}) custom-call(bf16[576,128]{1,0:T(8,128)(2,1)} %bitcast.11, bf16[128,3072]{1,0:T(8,128)(2,1)} %bitcast.8, bf16[128,2048]{1,0:T(8,128)(2,1)} %bitcast.9, s32[1,128]{1,0:T(1,128)} %seg_in.1, bf16[128,2048]{1,0:T(8,128)(2,1)} %wk_in.1, ...), custom_call_target="tpu_custom_call" | custom-call | tf_op jit(solution)/shard_map/pallas_call | solution.py:356
  60.1 1.7 %copy.9 = bf16[1,128,576]{1,2,0:T(8,128)(2,1)} copy(bf16[1,128,576]{2,1,0:T(8,128)(2,1)} %bitcast.10) | data formatting | bytes 294912
  61.8 0.0 copy-start
  61.8 2.1 %copy.12 = bf16[1,128,3072]{2,1,0:T(8,128)(2,1)} copy(bf16[1,128,3072]{2,1,0:T(8,128)(2,1)} %bitcast.7) | data formatting | bytes 1572864
  63.9 0.0 copy-done
  63.9 0.6 copy.13
Async XLA Ops:
  61.8 2.1 %copy-start = (f32[4,2048]{1,0:T(4,128)S(1)}, f32[4,2048]{1,0:T(4,128)}, u32[]{:S(2)}) copy-start(f32[4,2048]{1,0:T(4,128)} %get-tuple-element.17) | copy-start | bytes 98308

commit v3 on v2

--- a/solution.py
+++ b/solution.py
@@ -325,16 +325,17 @@
     h3 = [push(fl, lg_out.at[rows(y * 32, 32)], at(y_to=(y + dy) % 4)) for dy in (1, 2, 3)]
     l_fl = local(fl, lg_out.at[rows(y * 32, 32)])
 
-    for copy in over_z:
-        copy.wait_recv()
-    for k in range(4):
-        i = turns.index(k)
-        other = turns.index((k + 2) % 4)
-        total = tz[z, i].astype(F32)
-        for d in range(1, 16):
-            total = total + zr[d, i if d % 2 == 0 else other].astype(F32)
-        ksum[:, cols(order[k] * 256, 128)] = total[:8]
-        ksum[:, cols(order[k] * 256 + 128, 128)] = total[8:]
+    for ks, arriving in (((0, 2), over_z[:30]), ((1, 3), over_z[30:])):
+        for copy in arriving:
+            copy.wait_recv()
+        for k in ks:
+            i = turns.index(k)
+            other = turns.index((k + 2) % 4)
+            total = tz[z, i].astype(F32)
+            for d in range(1, 16):
+                total = total + zr[d, i if d % 2 == 0 else other].astype(F32)
+            ksum[:, cols(order[k] * 256, 128)] = total[:8]
+            ksum[:, cols(order[k] * 256 + 128, 128)] = total[8:]
     swap = push(ksum, kpeer, pair)
     ku_out[:, cols(c * 1024, 1024)] = jnp.where(c == 0, ksum[:4, :], ksum[4:, :])
     swap.wait_recv()
@@ -347,6 +348,28 @@
         kept.wait()
     for copy in sends:
         copy.wait_send()
+
+
+def deliver(qg_in, lg_in, ku_in, qg_out, lg_out, ku_out, qg, lg, lgt, ku, sem):
+    def copy(src, dst, i):
+        started = pltpu.make_async_copy(src, dst, sem.at[i])
+        started.start()
+        return started
+
+    parts = [pl.ds(16 * i, 16) for i in range(8)]
+    latent = copy(lg_in, lg, 0)
+    sums = copy(ku_in, ku, 1)
+    queries = [copy(qg_in.at[part], qg.at[part], 2 + i) for i, part in enumerate(parts)]
+    latent.wait()
+    lgt[...] = lg[...].T
+    out = [copy(lgt, lg_out, 10)]
+    sums.wait()
+    out.append(copy(ku, ku_out, 11))
+    for i, part in enumerate(parts):
+        queries[i].wait()
+        out.append(copy(qg.at[part], qg_out.at[part], 12 + i))
+    for started in out:
+        started.wait()
 
 
 def local_part(latent, queries, out_grad, segment_ids, key_up, value_up):
@@ -386,7 +409,22 @@
             collective_id=0, has_side_effects=True, vmem_limit_bytes=60 * 1024 * 1024
         ),
     )(latent[0].T, queries[0], out_grad[0], segment_ids, key_up, value_up)
-    return outs[0][None], outs[1][None], outs[2]
+    query_grad, latent_grad, key_up_grad = pl.pallas_call(
+        deliver,
+        out_shape=(
+            jax.ShapeDtypeStruct((128, 3072), BF16),
+            jax.ShapeDtypeStruct((576, 128), BF16),
+            jax.ShapeDtypeStruct((4, 2048), F32),
+        ),
+        in_specs=[hbm] * 3,
+        out_specs=[hbm] * 3,
+        scratch_shapes=[
+            V((128, 3072), BF16), V((128, 576), BF16), V((576, 128), BF16), V((4, 2048), F32),
+            pltpu.SemaphoreType.DMA((20,)),
+        ],
+        compiler_params=pltpu.CompilerParams(vmem_limit_bytes=60 * 1024 * 1024),
+    )(*outs)
+    return query_grad[None], latent_grad.T[None], key_up_grad
 
 
 def solution(mesh):

time: 64.6 us -> 62.4 us (0.966)
  local copies, waits for them, and re-layouts: 4.38 us -> 0 us
  Pallas kernels: 59.5 us -> 61.6 us
    unnamed x5 -> x0, local copies, waits for them, and re-layouts: 4.38 us -> none
    pallas_call x0 -> x1, Pallas kernels: none -> 2.11 us  [local_part(): pl.pallas_call(deliver, out_shape=(jax.ShapeDtypeStruct((128, 3072), BF16...]
where the time goes in v3:
time: 62.4 us; the launch traced here: 62.2 us
  Pallas kernels  61.6 us (99%)
  between operations  0.64 us (1%)
    pallas_call x1, Pallas kernels, local_part(): pl.pallas_call(kernel, out_shape=(jax.ShapeDtypeStruct((128, 3072), BF16)...  59.5 us
    pallas_call x1, Pallas kernels, local_part(): pl.pallas_call(deliver, out_shape=(jax.ShapeDtypeStruct((128, 3072), BF16...  2.11 us

profile of v3, /device:TPU:1, one launch (start us, length us, event | category | flops | bytes accessed | tf_op | source)
XLA Modules:
  0.0 62.2 jit_solution(16471293476057738483)
XLA Ops:
  0.6 59.5 %shard_map.85 = (bf16[128,3072]{1,0:T(8,128)(2,1)}, bf16[128,576]{1,0:T(8,128)(2,1)}, f32[4,2048]{1,0:T(4,128)}) custom-call(bf16[576,128]{1,0:T(8,128)(2,1)} %bitcast.11, bf16[128,3072]{1,0:T(8,128)(2,1)} %bitcast.9, bf16[128,2048]{1,0:T(8,128)(2,1)} %bitcast.10, s32[1,128]{1,0:T(1,128)} %seg_in.1, bf16[128,2048]{1,0:T(8,128)(2,1)} %wk_in.1, ...), custom_call_target="tpu_custom_call" | custom-call | tf_op jit(solution)/shard_map/pallas_call | solution.py:379
  60.1 2.1 %shard_map.86 = (bf16[128,3072]{1,0:T(8,128)(2,1)}, bf16[576,128]{1,0:T(8,128)(2,1)}, f32[4,2048]{1,0:T(4,128)}) custom-call(bf16[128,3072]{1,0:T(8,128)(2,1)} %get-tuple-element.9.qg_in, bf16[128,576]{1,0:T(8,128)(2,1)} %get-tuple-element.10.lg_in, f32[4,2048]{1,0:T(4,128)} %get-tuple-element.11.ku_in), custom_call_target="tpu_custom_call" | custom-call | tf_op jit(solution)/shard_map/pallas_call | solution.py:412

commit v4 on v3

--- a/solution.py
+++ b/solution.py
@@ -37,7 +37,7 @@
     qg_out, lg_out, ku_out,
     wk, wv, qs, gs, latt, lat, seg, bias, ctp, to_owner, rope0, rope1, kx, vx, dq, u, lacc, racc, dkp, dvp,
     ux, tz, zr, ksum, kpeer, lb, p1, l2, p2, fl,
-    send_sem, recv_sem, local_sem,
+    send_sem, recv_sem, local_sem, known_sem,
 ):
     s = lax.axis_index("ctx")
     y = lax.axis_index("head")
@@ -83,7 +83,7 @@
         return copy
 
     partners = [pair, at(x_to=right), at(x_to=left), at(x_to=far)]
-    partners += [at(dz=d) for d in range(1, 16)]
+    partners += [at(dz=d) for d in (1, -1, 2, -2)]
     for dy in (1, 2, 3):
         yt = (y + dy) % 4
         partners += [at(y_to=yt), at(dz=-1, y_to=yt), at(dz=1, y_to=yt)]
@@ -111,6 +111,14 @@
     racc[...] = jnp.zeros_like(racc)
     pl.semaphore_wait(barrier, len(partners))
 
+    def tell(i, reach):
+        for d in (reach, -reach):
+            pl.semaphore_signal(
+                known_sem.at[i], inc=1, device_id=at(dz=d), device_id_type=pl.DeviceIdType.MESH
+            )
+
+    tell(0, 2)
+
     def push_direct(k):
         p = order[k]
         out = []
@@ -158,6 +166,9 @@
         tokens.append(push_tokens(k))
 
     zf = {(0, 0): forward_z(0, 0)}
+
+    pl.semaphore_wait(known_sem.at[0], 2)
+    tell(1, 4)
 
     l_seg.wait()
     seg_p.wait_recv()
@@ -276,6 +287,7 @@
         return lambda: over_x.append(push_x(k))
 
     compute(0, lambda: None, pushed_x(0))
+    pl.semaphore_wait(known_sem.at[1], 2)
     zf[1, 0] = forward_z(1, 0)
     queries.append(push_queries(0))
     for part in range(2):
@@ -326,6 +338,12 @@
     l_fl = local(fl, lg_out.at[rows(y * 32, 32)])
 
     for ks, arriving in (((0, 2), over_z[:30]), ((1, 3), over_z[30:])):
+        if ks == (1, 3):
+            for moved, kept in queries:
+                moved.wait_recv()
+                kept.wait()
+            for copy in sends:
+                copy.wait_send()
         for copy in arriving:
             copy.wait_recv()
         for k in ks:
@@ -343,11 +361,7 @@
     for copy in h3:
         copy.wait_recv()
     l_fl.wait()
-    for moved, kept in queries:
-        moved.wait_recv()
-        kept.wait()
-    for copy in sends:
-        copy.wait_send()
+    swap.wait_send()
 
 
 def deliver(qg_in, lg_in, ku_in, qg_out, lg_out, ku_out, qg, lg, lgt, ku, sem):
@@ -404,6 +418,7 @@
             pltpu.SemaphoreType.DMA((N_REMOTE,)),
             pltpu.SemaphoreType.DMA((N_REMOTE,)),
             pltpu.SemaphoreType.DMA((N_LOCAL,)),
+            pltpu.SemaphoreType.REGULAR((2,)),
         ],
         compiler_params=pltpu.CompilerParams(
             collective_id=0, has_side_effects=True, vmem_limit_bytes=60 * 1024 * 1024

time: 62.4 us -> 60.4 us (0.968)
  Pallas kernels: 61.6 us -> 59.7 us
    pallas_call x1, Pallas kernels: 59.5 us -> 57.5 us  [local_part(): pl.pallas_call(kernel, out_shape=(jax.ShapeDtypeStruct((128, 3072), BF16)...]
where the time goes in v4:
time: 60.4 us; the launch traced here: 60.3 us
  Pallas kernels  59.7 us (99%)
  between operations  0.64 us (1%)
    pallas_call x1, Pallas kernels, local_part(): pl.pallas_call(kernel, out_shape=(jax.ShapeDtypeStruct((128, 3072), BF16)...  57.5 us
    pallas_call x1, Pallas kernels, local_part(): pl.pallas_call(deliver, out_shape=(jax.ShapeDtypeStruct((128, 3072), BF16...  2.11 us

profile of v4, /device:TPU:1, one launch (start us, length us, event | category | flops | bytes accessed | tf_op | source)
XLA Modules:
  0.0 60.3 jit_solution(4865009604612249572)
XLA Ops:
  0.6 57.5 %shard_map.85 = (bf16[128,3072]{1,0:T(8,128)(2,1)}, bf16[128,576]{1,0:T(8,128)(2,1)}, f32[4,2048]{1,0:T(4,128)}) custom-call(bf16[576,128]{1,0:T(8,128)(2,1)} %bitcast.11, bf16[128,3072]{1,0:T(8,128)(2,1)} %bitcast.9, bf16[128,2048]{1,0:T(8,128)(2,1)} %bitcast.10, s32[1,128]{1,0:T(1,128)} %seg_in.1, bf16[128,2048]{1,0:T(8,128)(2,1)} %wk_in.1, ...), custom_call_target="tpu_custom_call" | custom-call | tf_op jit(solution)/shard_map/pallas_call | solution.py:393
  58.2 2.1 %shard_map.86 = (bf16[128,3072]{1,0:T(8,128)(2,1)}, bf16[576,128]{1,0:T(8,128)(2,1)}, f32[4,2048]{1,0:T(4,128)}) custom-call(bf16[128,3072]{1,0:T(8,128)(2,1)} %get-tuple-element.9.qg_in, bf16[128,576]{1,0:T(8,128)(2,1)} %get-tuple-element.10.lg_in, f32[4,2048]{1,0:T(4,128)} %get-tuple-element.11.ku_in), custom_call_target="tpu_custom_call" | custom-call | tf_op jit(solution)/shard_map/pallas_call | solution.py:427
